TPU v7x, 512 devices: a whole 4x8x8 slice. The times are simulated.
512 devices in a mesh: rep: 8 (over y_hi, core), ep: 64 (over y_lo, z, x).
Axes of the slice: x: 4, y: 8 (y_hi: 4, y_lo: 2; y = y_hi * 2 + y_lo), z: 8, core: 2. Of those that a mesh axis runs over, the one named last changes fastest.
Arguments:
- dense_grad: float32 [8, 64, 128, 7168], P('rep', 'ep'), may hold values from -16 to 16
- dense_param: float32 [128, 7168], P('ep'), may hold values from -5 to 5
- dense_first: float32 [128, 7168], P('ep'), may hold values from -128 to 128
- dense_second: float32 [128, 7168], P('ep'), may hold values from 20 to 2000
- expert_grad: float32 [8, 1024, 7168], P('rep', 'ep'), may hold values from -6 to 6
- expert_param: float32 [1024, 7168], P('ep'), may hold values from -5 to 5
- expert_first: float32 [1024, 7168], P('ep'), may hold values from -16 to 16
- expert_second: float32 [1024, 7168], P('ep'), may hold values from 0.5 to 50
Outputs:
- new_dense: float32 [128, 7168], replicated
- new_expert: float32 [1024, 7168], P('ep')
All inputs are finite; a program needn't handle non-finite values.
Results may differ from a plain program's by a relative error of at most 0.00002.
Values sent between devices are 32-bit elements; how exact they have to be, the bound alone decides.
A program may use at most 64 MiB of HBM per device.

v0:
```python
import jax
import jax.numpy as jnp
from jax import lax
from jax.sharding import PartitionSpec as P

beta_one = 0.9
beta_two = 0.95
corr_one = 0.19
corr_two = 0.0975
learn_rate = 0.2
decay_rate = 0.1
epsilon = 1e-08


def adamw(grad, param, first, second):
    first_new = beta_one * first + (1.0 - beta_one) * grad
    second_new = beta_two * second + (1.0 - beta_two) * grad * grad
    step_dir = first_new / corr_one / (jnp.sqrt(second_new / corr_two) + epsilon)
    return param - learn_rate * (step_dir + decay_rate * param)


def shards(
    dense_grad,
    dense_param,
    dense_first,
    dense_second,
    expert_grad,
    expert_param,
    expert_first,
    expert_second,
):
    expert_total = lax.psum(expert_grad[0], "rep")
    new_expert = adamw(expert_total, expert_param, expert_first, expert_second)
    dense_rows_sum = lax.psum_scatter(dense_grad[0, 0], "ep", scatter_dimension=0, tiled=True)
    dense_total = lax.psum(dense_rows_sum, "rep")
    updated = adamw(dense_total, dense_param, dense_first, dense_second)
    new_dense = lax.all_gather(updated, "ep", axis=0, tiled=True)
    return (new_dense, new_expert)


def solution(mesh):
    placed = (
        P("rep", "ep", None, None),
        P("ep", None),
        P("ep", None),
        P("ep", None),
        P("rep", "ep", None),
        P("ep", None),
        P("ep", None),
        P("ep", None),
    )
    return jax.shard_map(
        shards, mesh=mesh, in_specs=placed, out_specs=(P(), P("ep", None)), check_vma=False
    )
```

profile of v0, /device:TPU:8, one launch (start us, length us, event | category | flops | bytes accessed | tf_op | source)
XLA Modules:
  0.0 1035.9 jit_solution(17649942808138937762)
XLA Ops:
  7.2 0.0 copy-start.5
  7.2 0.0 copy-start.4
  7.2 0.0 copy-start.3
  7.2 0.0 copy-start
  7.2 0.0 copy-start.2
  7.2 0.0 copy-start.1
  7.2 0.0 all-reduce.6.cloned.1.call-start
  7.3 0.7 all-reduce.6.cloned.1.call-update
  8.0 0.0 all-reduce.4.cloned.1.call-start
  8.0 0.7 all-reduce.4.cloned.1.call-update
  8.7 0.0 all-gather.3.cloned.1.call-start
  8.8 1.3 dynamic-slice
  10.7 625.7 %all-reduce.6.cloned.1.call-done = f32[128,7168]{1,0:T(8,128)} async-done(((f32[128,7168]{1,0:T(8,128)}), f32[128,7168]{1,0:T(8,128)}) %all-reduce.6.cloned.1.call-update) | async-done | bytes 3670032
  636.3 1.0 constant_dynamic-slice_fusion
  637.3 27.9 %psum.14 = f32[2,7168]{1,0:T(2,128)S(1)} all-reduce(f32[2,7168]{1,0:T(2,128)S(1)} %constant_dynamic-slice_fusion), channel_id=1, replica_groups=mesh['rep'=8,'ep'=64] {'rep'}, use_global_device_ids=true, to_apply=%region_1.0 | all-reduce | flops 14336 | bytes 114688 | tf_op jit(solution)/shard_map/psum | solution.py:35
  665.3 0.0 copy-done.5
  665.3 0.0 copy-done.4
  665.3 0.0 copy-done.3
  665.3 0.8 subtract_bitcast_fusion
  666.1 0.0 all-gather.3.cloned.1.call-update
  666.1 49.9 %all-reduce.4.cloned.1.call-done = f32[16,7168]{1,0:T(8,128)} async-done(((f32[16,7168]{1,0:T(8,128)}), f32[16,7168]{1,0:T(8,128)}) %all-reduce.4.cloned.1.call-update) | async-done | bytes 458768 | tf_op jit(solution)/shard_map/psum | solution.py:32
  716.0 0.0 copy-done
  716.0 0.0 copy-done.2
  716.0 0.0 copy-done.1
  716.0 2.1 multiply_subtract_fusion
  718.2 305.5 %all-gather.3.cloned.1.call-done = f32[64,2,7168]{2,1,0:T(2,128)} async-done(((f32[1,2,7168]{2,1,0:T(2,128)}), f32[64,2,7168]{2,1,0:T(2,128)}) %all-gather.3.cloned.1.call-update) | async-done | bytes 3670032 | tf_op jit(solution)/shard_map/all_gather | solution.py:37
  1023.7 5.6 reshape.5
Async XLA Ops:
  7.2 658.1 %copy-start.5 = (f32[2,7168]{1,0:T(2,128)S(1)}, f32[2,7168]{1,0:T(2,128)}, u32[]{:S(2)}) copy-start(f32[2,7168]{1,0:T(2,128)} %param.10) | copy-start | bytes 172036
  7.2 658.1 %copy-start.4 = (f32[2,7168]{1,0:T(2,128)S(1)}, f32[2,7168]{1,0:T(2,128)}, u32[]{:S(2)}) copy-start(f32[2,7168]{1,0:T(2,128)} %param.11) | copy-start | bytes 172036
  7.2 658.1 %copy-start.3 = (f32[2,7168]{1,0:T(2,128)S(1)}, f32[2,7168]{1,0:T(2,128)}, u32[]{:S(2)}) copy-start(f32[2,7168]{1,0:T(2,128)} %param.9) | copy-start | bytes 172036
  7.2 708.8 %copy-start = (f32[16,7168]{1,0:T(8,128)S(1)}, f32[16,7168]{1,0:T(8,128)}, u32[]{:S(2)}) copy-start(f32[16,7168]{1,0:T(8,128)} %param.13) | copy-start | bytes 1376260
  7.2 708.8 %copy-start.2 = (f32[16,7168]{1,0:T(8,128)S(1)}, f32[16,7168]{1,0:T(8,128)}, u32[]{:S(2)}) copy-start(f32[16,7168]{1,0:T(8,128)} %param.14) | copy-start | bytes 1376260
  7.2 708.8 %copy-start.1 = (f32[16,7168]{1,0:T(8,128)S(1)}, f32[16,7168]{1,0:T(8,128)}, u32[]{:S(2)}) copy-start(f32[16,7168]{1,0:T(8,128)} %param.15) | copy-start | bytes 1376260
  7.2 629.1 %all-reduce.6.cloned.1.call-start = ((), (), s32[]{:S(2)}) async-start(), calls=%async_computation.2 | async-start | bytes 7340032
  8.0 708.1 %all-reduce.4.cloned.1.call-start = ((), (), s32[]{:S(2)}) async-start(), calls=%async_computation | async-start | bytes 917504 | tf_op jit(solution)/shard_map/psum | solution.py:32
  8.7 1015.0 %all-gather.3.cloned.1.call-start = ((), (), s32[]{:S(2)}) async-start(), calls=%async_computation.1 | async-start | bytes 3727360 | tf_op jit(solution)/shard_map/all_gather | solution.py:37
Sparse Core Ops, SparseCore 0:
  11.0 625.3 all-reduce.5
  639.5 76.4 all-reduce.3
  718.7 304.9 all-gather.2
where the time goes:
time: 1040 us
  waiting for transfers between devices  982 us (94%)
  blocking collectives  27.9 us (3%)
  between operations  14.5 us (1%)
    unnamed x4, waiting for transfers between devices  627 us
    all_gather x1, waiting for transfers between devices, shards(): new_dense = lax.all_gather(updated, 'ep', axis=0, tiled=True)  306 us
    psum x1, waiting for transfers between devices, shards(): expert_total = lax.psum(expert_grad[0], 'rep')  49.9 us
    psum x1, blocking collectives, shards(): dense_total = lax.psum(dense_rows_sum, 'rep')  27.9 us
  transfers between devices with their start and end apart: 3, of which 3 were waited for; matrix products, arithmetic and copies ran while one was open for 0% of the time, Pallas kernels for 0%

commit v1 on v0

v1 whole, which is shorter than its diff:
```python
import jax
import jax.numpy as jnp
from jax import lax
from jax.experimental import pallas as pl
from jax.experimental.pallas import tpu as pltpu
from jax.sharding import PartitionSpec as P

MESH = pl.DeviceIdType.MESH
D = 7168
T = 128


def adamw(grad, param, first, second):
    first_new = 0.9 * first + (1.0 - 0.9) * grad
    second_new = 0.95 * second + (1.0 - 0.95) * grad * grad
    step_dir = first_new / 0.19 / (jnp.sqrt(second_new / 0.0975) + 1e-08)
    return param - 0.2 * (step_dir + 0.1 * param)


def tiles(start, count):
    first = start * T
    if not isinstance(first, int):
        first = pl.multiple_of(first, T)
    return pl.ds(first, count * T)


def eight(index):
    return pl.ds(pl.multiple_of(index * 8, 8), 8)


def kernel(
    grad, param, first, second, egrad, eparam, efirst, esecond,
    out, eout,
    g_a, p_a, g_c, p_c, g_b, p_b, g_e, p_e,
    r_a1, s_a, r_a2y, t_ay, r_a2z, t_az, r_a3,
    r_c1, s_c, r_c2, t_c, r_c3,
    r_b1, s_b, r_b2, t_b, r_b3,
    r_e, ep_buf, state, gathered, packed,
    load_sem, send_sem, recv_sem,
):
    rep, ep = lax.axis_index("rep"), lax.axis_index("ep")
    core = lax.rem(rep, 2)
    x, z = lax.rem(ep, 4), lax.rem(ep // 4, 8)
    yh, yl = rep // 2, ep // 32
    y = yh * 2 + yl

    def at(xx, yy, zz, cc):
        return {"rep": (yy // 2) * 2 + cc, "ep": lax.rem(yy, 2) * 32 + zz * 4 + xx}

    def x_peer(d):
        return at(lax.rem(x + d, 4), y, z, core)

    def y_peer(d):
        return at(x, lax.rem(y + d, 8), z, core)

    def z_peer(d):
        return at(x, y, lax.rem(z + d, 8), core)

    partner = at(x, y, z, 1 - core)

    barrier = pltpu.get_barrier_semaphore()
    peers = [partner] + [x_peer(d) for d in range(1, 4)]
    peers += [f(d) for d in range(1, 8) for f in (y_peer, z_peer)]
    for peer in peers:
        pl.semaphore_signal(barrier, inc=1, device_id=peer, device_id_type=MESH)

    def body(c):
        n_load, n_sem = [0], [0]
        sent = []

        def load(src, dst):
            copy = pltpu.make_async_copy(src, dst, load_sem.at[n_load[0]])
            n_load[0] += 1
            copy.start()
            return copy

        def link(src, dst, device):
            k = n_sem[0]
            n_sem[0] += 1
            return pltpu.make_async_remote_copy(
                src, dst, send_sem.at[k], recv_sem.at[k], device_id=device, device_id_type=MESH
            )

        def send(src, dst, device):
            copy = link(src, dst, device)
            copy.start()
            sent.append(copy)
            return copy

        o = 1 - c
        order = [lax.rem(x + d, 4) for d in (2, 1, 3, 0)]
        own_a, own_c, own_b, own_e = [], None, None, None
        for xx in order:
            own_a.append(load(grad.at[:, :, tiles(c * 16 + xx * 4, 4)], g_a.at[xx]))
        own_c = load(grad.at[:, :, tiles(32 + c * 8, 8)], g_c)
        own_b = load(grad.at[:, :, tiles(48 + c * 4, 4)], g_b)
        own_e = load(egrad.at[:, tiles(c * 28, 28)], g_e)
        e_cols = tiles(c * 28 + yh * 7, 7)
        own_s = [load(r, state.at[i]) for i, r in enumerate((param, first, second))]
        own_ep = [load(r.at[:, e_cols], ep_buf.at[i]) for i, r in enumerate((eparam, efirst, esecond))]
        for copy in own_s:
            copy.wait()

        pl.semaphore_wait(barrier, len(peers))

        part_a = []
        for i, xx in enumerate(order):
            part_a.append(send(grad.at[:, :, tiles(o * 16 + xx * 4, 4)], p_a.at[xx], partner))
            if i == 0:
                part_c = send(grad.at[:, :, tiles(32 + o * 8, 8)], p_c, partner)
            if i == 1:
                part_b = send(grad.at[:, :, tiles(48 + o * 4, 4)], p_b, partner)
                part_e = send(egrad.at[:, tiles(o * 28, 28)], p_e, partner)

        def state_tiles(xx):
            jj = lax.rem(y, 4) // 2
            return (c * 16 + xx * 4 + yh, 32 + c * 8 + xx * 2 + jj, 48 + c * 4 + yh)

        state_recv = []
        for d in range(1, 4):
            for i, ct in enumerate(state_tiles(lax.rem(x + d, 4))):
                state_recv.append(send(state.at[:, :, tiles(ct, 1)], gathered.at[d, i], x_peer(d)))

        def piece(ref, p):
            if c == 0:
                return ref.at[lax.rem(p, 2), :, tiles(p // 2, 1)]
            return ref.at[:, eight(p), :]

        def a_send(i, xx, d):
            own_a[i].wait()
            part_a[i].wait_recv()
            g_a[xx] = g_a[xx] + p_a[xx]
            if d == 0:
                return None
            mid = y if c == 0 else z
            return [
                send(piece(g_a.at[xx], lax.rem(mid + k, 8)), piece(r_a1.at[d - 1], lax.rem(mid + k, 8)), x_peer(d))
                for k in range(8)
            ]

        a1 = {}
        a1[2] = a_send(0, order[0], 2)

        own_c.wait()
        part_c.wait_recv()
        g_c[...] = g_c[...] + p_c[...]
        c1 = [
            send(g_c.at[:, eight(lax.rem(z + d, 8)), :], r_c1.at[d - 1], z_peer(d)) for d in range(1, 8)
        ]

        a1[1] = a_send(1, order[1], 1)

        own_b.wait()
        part_b.wait_recv()
        g_b[...] = g_b[...] + p_b[...]
        b1 = []
        for d in range(1, 8):
            yy = lax.rem(y + d, 8)
            b1.append(send(g_b.at[lax.rem(yy, 2), :, tiles(yy // 2, 1)], r_b1.at[d - 1], y_peer(d)))

        own_e.wait()
        part_e.wait_recv()
        g_e[...] = g_e[...] + p_e[...]
        e1 = [
            send(g_e.at[:, tiles(lax.rem(yh + d, 4) * 7, 7)], r_e.at[d - 1], y_peer(2 * d)) for d in range(1, 4)
        ]

        a1[3] = a_send(2, order[2], 3)
        a_send(3, order[3], 0)

        for copy in state_recv:
            copy.wait_recv()
        for i, ct in enumerate(state_tiles(x)):
            for d in range(4):
                row = pl.ds(2 * lax.rem(x + 4 - d, 4), 2)
                for j in range(3):
                    if d == 0:
                        packed[i, j, row, :] = state[j, :, tiles(ct, 1)]
                    else:
                        packed[i, j, row, :] = gathered[d, i, j]

        mid = y if c == 0 else z
        second_a, r_a2, t_a = ([], r_a2y, t_ay) if c == 0 else ([], r_a2z, t_az)
        mid_peer, last_peer = (y_peer, z_peer) if c == 0 else (z_peer, y_peer)
        for k in (1, 2, 3, 4, 5, 6, 7, 0):
            p = lax.rem(mid + k, 8)
            for d in (2, 1, 3):
                a1[d][k].wait_recv()
            total = piece(g_a.at[x], p)[...]
            for d in (1, 2, 3):
                total = total + piece(r_a1.at[d - 1], p)[...]
            if k:
                piece(s_a, p)[...] = total
                second_a.append(send(piece(s_a, p), r_a2.at[k - 1], mid_peer(k)))
            else:
                t_a[...] = total

        for copy in c1:
            copy.wait_recv()
        total = g_c[:, eight(z), :]
        for d in range(1, 8):
            total = total + r_c1[d - 1]
        s_c[...] = total
        c2 = [
            send(s_c.at[:, :, tiles(2 * lax.rem(x + d, 4), 2)], r_c2.at[d - 1], x_peer(d)) for d in range(1, 4)
        ]

        for copy in b1:
            copy.wait_recv()
        total = g_b[yl, :, tiles(yh, 1)]
        for d in range(1, 8):
            total = total + r_b1[d - 1]
        s_b[...] = total
        b2 = [send(s_b.at[eight(lax.rem(z + d, 8)), :], r_b2.at[d - 1], z_peer(d)) for d in range(1, 8)]

        for copy in e1:
            copy.wait_recv()
        for copy in own_ep:
            copy.wait()
        total = g_e[:, tiles(yh * 7, 7)]
        for d in range(1, 4):
            total = total + r_e[d - 1]
        eout[:, e_cols] = adamw(total, ep_buf[0], ep_buf[1], ep_buf[2])
        e2 = [send(eout.at[:, e_cols], eout.at[:, e_cols], y_peer(2 * d)) for d in range(1, 4)]
        e_done = [send(eout.at[:, e_cols], eout.at[:, e_cols], partner)]

        for copy in second_a:
            copy.wait_recv()
        total = t_a[...]
        for d in range(1, 8):
            total = total + r_a2[d - 1]
        t_a[...] = total
        a3 = []
        for d in range(1, 8):
            if c == 0:
                src = t_a.at[eight(lax.rem(z + d, 8)), :]
            else:
                yy = lax.rem(y + d, 8)
                src = t_a.at[lax.rem(yy, 2), :, tiles(yy // 2, 1)]
            a3.append(send(src, r_a3.at[d - 1], last_peer(d)))

        for copy in c2:
            copy.wait_recv()
        total = s_c[:, :, tiles(2 * x, 2)]
        for d in range(1, 4):
            total = total + r_c2[d - 1]
        t_c[...] = total
        c_first = 4 * lax.rem(x, 2)

        def c_owner(d):
            yy = lax.rem(y + d, 8)
            return yy // 4 == lax.rem(x, 2), yy

        c3 = []
        for d in range(1, 8):
            owns, yy = c_owner(d)
            copy = link(t_c.at[lax.rem(yy, 2), :, tiles(lax.rem(yy, 4) // 2, 1)], r_c3.at[d - 1], y_peer(d))
            c3.append(copy)

            @pl.when(owns)
            def _(copy=copy):
                copy.start()

        for copy in b2:
            copy.wait_recv()
        total = s_b[eight(z), :]
        for d in range(1, 8):
            total = total + r_b2[d - 1]
        t_b[...] = total
        b3 = []
        for d in range(1, 4):
            copy = link(t_b, r_b3.at[d - 1], x_peer(d))
            b3.append(copy)

            @pl.when(lax.rem(x + d, 4) == yh)
            def _(copy=copy):
                copy.start()

        for copy in a3:
            copy.wait_recv()
        total = t_a[eight(z), :] if c == 0 else t_a[yl, :, tiles(yh, 1)]
        for d in range(1, 8):
            total = total + r_a3[d - 1]
        ct_a, ct_c, ct_b = state_tiles(x)
        tile_a = out.at[yl, eight(z), tiles(ct_a, 1)]
        tile_a[...] = adamw(total, packed[0, 0], packed[0, 1], packed[0, 2])
        a4 = [send(tile_a, tile_a, last_peer(d)) for d in range(1, 8)]

        tile_c = out.at[yl, eight(z), tiles(ct_c, 1)]
        c4 = [link(tile_c, tile_c, y_peer(d)) for d in range(1, 8)]
        mine_c = y // 4 == lax.rem(x, 2)

        @pl.when(mine_c)
        def _():
            for copy in c3:
                copy.wait_recv()
            total = t_c[yl, :, tiles(lax.rem(y, 4) // 2, 1)]
            for d in range(1, 8):
                total = total + r_c3[d - 1]
            tile_c[...] = adamw(total, packed[1, 0], packed[1, 1], packed[1, 2])
            for copy in c4:
                copy.start()

        tile_b = out.at[yl, eight(z), tiles(ct_b, 1)]
        b4 = [link(tile_b, tile_b, x_peer(d)) for d in range(1, 4)]
        mine_b = x == yh

        @pl.when(mine_b)
        def _():
            for copy in b3:
                copy.wait_recv()
            total = t_b[...]
            for d in range(1, 4):
                total = total + r_b3[d - 1]
            tile_b[...] = adamw(total, packed[2, 0], packed[2, 1], packed[2, 2])
            for copy in b4:
                copy.start()

        for d in range(1, 4):
            e2[d - 1].wait_recv()
            cols = tiles(c * 28 + lax.rem(yh + 4 - d, 4) * 7, 7)
            e_done.append(send(eout.at[:, cols], eout.at[:, cols], partner))

        for copy in a4:
            copy.wait_recv()
        block_a = out.at[:, :, tiles(c * 16 + x * 4, 4)]
        mine = piece(block_a, mid)
        a5 = [send(mine, mine, mid_peer(d)) for d in range(1, 8)]
        done = []
        a6 = {1: [], 2: [], 3: []}
        for d in (2, 1, 3):
            a6[d].append(send(mine, mine, x_peer(d)))
        done.append(send(mine, mine, partner))

        for d in range(1, 4):
            @pl.when(lax.rem(x + 4 - d, 4) == yh)
            def _(copy=b4[d - 1]):
                copy.wait_recv()
        b5 = [send(tile_b, tile_b, z_peer(d)) for d in range(1, 8)]

        for d in range(1, 8):
            @pl.when(lax.rem(y + 8 - d, 8) // 4 == lax.rem(x, 2))
            def _(copy=c4[d - 1]):
                copy.wait_recv()
        block_c = out.at[:, eight(z), tiles(32 + c * 8 + x * 2, 2)]
        c5 = [send(block_c, block_c, x_peer(d)) for d in range(1, 4)]

        for copy in b5:
            copy.wait_recv()
        col_b = out.at[yl, :, tiles(ct_b, 1)]
        b6 = [send(col_b, col_b, y_peer(d)) for d in range(1, 8)]

        for copy in c5:
            copy.wait_recv()
        row_c = out.at[:, eight(z), tiles(32 + c * 8, 8)]
        c6 = [send(row_c, row_c, z_peer(d)) for d in range(1, 8)]

        for k in range(1, 8):
            a5[k - 1].wait_recv()
            got = piece(block_a, lax.rem(mid + 8 - k, 8))
            for d in (2, 1, 3):
                a6[d].append(send(got, got, x_peer(d)))
            done.append(send(got, got, partner))

        for copy in b6:
            copy.wait_recv()
        all_b = out.at[:, :, tiles(48 + c * 4, 4)]
        done.append(send(all_b, all_b, partner))
        for k in range(8):
            for d in (1, 3, 2):
                a6[d][k].wait_recv()
                got = piece(out.at[:, :, tiles(c * 16 + lax.rem(x + 4 - d, 4) * 4, 4)], lax.rem(mid + 8 - k, 8))
                done.append(send(got, got, partner))
        for copy in c6:
            copy.wait_recv()
        all_c = out.at[:, :, tiles(32 + c * 8, 8)]
        done.append(send(all_c, all_c, partner))

        for copy in e_done + done:
            copy.wait_recv()
        for copy in sent:
            copy.wait_send()
        for d in range(1, 8):
            @pl.when(c_owner(d)[0])
            def _(copy=c3[d - 1]):
                copy.wait_send()
        for d in range(1, 4):
            @pl.when(lax.rem(x + d, 4) == yh)
            def _(copy=b3[d - 1]):
                copy.wait_send()

        @pl.when(mine_c)
        def _():
            for copy in c4:
                copy.wait_send()

        @pl.when(mine_b)
        def _():
            for copy in b4:
                copy.wait_send()

    for value in range(2):
        @pl.when(core == value)
        def _(value=value):
            body(value)


def shards(grad, param, first, second, egrad, eparam, efirst, esecond):
    vmem = lambda *shape: pltpu.VMEM(shape, jnp.float32)
    block = (2, 64, 4 * T)
    out, eout = pl.pallas_call(
        kernel,
        out_shape=(
            jax.ShapeDtypeStruct((2, 64, D), jnp.float32),
            jax.ShapeDtypeStruct((16, D), jnp.float32),
        ),
        in_specs=[pl.BlockSpec(memory_space=pl.ANY)] * 8,
        out_specs=(pl.BlockSpec(memory_space=pltpu.VMEM),) * 2,
        scratch_shapes=[
            vmem(4, *block), vmem(4, *block), vmem(2, 64, 8 * T), vmem(2, 64, 8 * T), vmem(*block), vmem(*block),
            vmem(16, 28 * T), vmem(16, 28 * T),
            vmem(3, *block), vmem(*block), vmem(7, 64, T), vmem(64, T), vmem(7, 2, 8, 4 * T), vmem(2, 8, 4 * T), vmem(7, 8, T),
            vmem(7, 2, 8, 8 * T), vmem(2, 8, 8 * T), vmem(3, 2, 8, 2 * T), vmem(2, 8, 2 * T), vmem(7, 8, T),
            vmem(7, 64, T), vmem(64, T), vmem(7, 8, T), vmem(8, T), vmem(3, 8, T),
            vmem(3, 16, 7 * T), vmem(3, 16, 7 * T), vmem(3, 2, D), vmem(4, 3, 3, 2, T), vmem(3, 3, 8, T),
            pltpu.SemaphoreType.DMA((16,)),
            pltpu.SemaphoreType.DMA((240,)),
            pltpu.SemaphoreType.DMA((240,)),
        ],
        compiler_params=pltpu.CompilerParams(
            collective_id=0, has_side_effects=True, vmem_limit_bytes=40 * 1024 * 1024
        ),
        name="reduce_update_gather",
    )(
        grad.reshape(2, 64, D), param, first, second,
        egrad.reshape(16, D), eparam, efirst, esecond,
    )
    return out.reshape(128, D), eout


def solution(mesh):
    placed = (
        P("rep", "ep", None, None),
        P("ep", None),
        P("ep", None),
        P("ep", None),
        P("rep", "ep", None),
        P("ep", None),
        P("ep", None),
        P("ep", None),
    )
    return jax.shard_map(
        shards, mesh=mesh, in_specs=placed, out_specs=(P(), P("ep", None)), check_vma=False
    )
```

time: 1040 us -> 83.4 us (0.08)
  the two profiles are of different devices: /device:TPU:8 before, /device:TPU:1 now
where the time goes in v1:
time: 83.4 us; the launch traced here: 82.9 us
  Pallas kernels  71.1 us (85%)
  local copies, waits for them, and re-layouts  11.2 us (13%)
    pallas_call x1, Pallas kernels, shards(): pl.pallas_call(kernel, out_shape=(jax.ShapeDtypeStruct((2, 64, D), jnp.fl...  71.1 us
    unnamed x18, local copies, waits for them, and re-layouts  11.2 us

profile of v1, /device:TPU:1, one launch (start us, length us, event | category | flops | bytes accessed | tf_op | source)
XLA Modules:
  0.0 82.9 jit_solution(1138479515698989209)
XLA Ops:
  0.6 0.0 copy-start
  0.6 2.0 %copy-done = f32[1,1,128,7168]{3,2,1,0:T(8,128)S(1)} copy-done((f32[1,1,128,7168]{3,2,1,0:T(8,128)S(1)}, f32[1,1,128,7168]{3,2,1,0:T(8,128)}, u32[]{:S(2)}) %copy-start) | copy-done | bytes 3670040
  2.7 0.0 copy-start.1
  2.7 1.0 %copy-done.1 = f32[1,16,7168]{2,1,0:T(8,128)S(1)} copy-done((f32[1,16,7168]{2,1,0:T(8,128)S(1)}, f32[1,16,7168]{2,1,0:T(8,128)}, u32[]{:S(2)}) %copy-start.1) | copy-done | bytes 458776
  3.7 0.0 copy-start.2
  3.7 1.0 %copy-done.2 = f32[16,7168]{1,0:T(8,128)S(1)} copy-done((f32[16,7168]{1,0:T(8,128)S(1)}, f32[16,7168]{1,0:T(8,128)}, u32[]{:S(2)}) %copy-start.2) | copy-done | bytes 458776
  4.7 0.0 copy-start.3
  4.7 1.0 %copy-done.3 = f32[16,7168]{1,0:T(8,128)S(1)} copy-done((f32[16,7168]{1,0:T(8,128)S(1)}, f32[16,7168]{1,0:T(8,128)}, u32[]{:S(2)}) %copy-start.3) | copy-done | bytes 458776
  5.7 0.0 copy-start.4
  5.7 1.0 %copy-done.4 = f32[16,7168]{1,0:T(8,128)S(1)} copy-done((f32[16,7168]{1,0:T(8,128)S(1)}, f32[16,7168]{1,0:T(8,128)}, u32[]{:S(2)}) %copy-start.4) | copy-done | bytes 458776
  6.7 0.0 copy-start.5
  6.8 0.8 copy-done.5
  7.6 0.0 copy-start.6
  7.6 0.8 copy-done.6
  8.4 0.0 copy-start.7
  8.4 0.8 copy-done.7
  9.2 71.1 %reduce_update_gather.1 = (f32[2,64,7168]{2,1,0:T(8,128)S(1)}, f32[16,7168]{1,0:T(8,128)S(1)}) custom-call(f32[2,64,7168]{2,1,0:T(8,128)S(1)} %bitcast.4, f32[2,7168]{1,0:T(2,128)S(1)} %copy-done.5, f32[2,7168]{1,0:T(2,128)S(1)} %copy-done.6, f32[2,7168]{1,0:T(2,128)S(1)} %copy-done.7, f32[16,7168]{1,0:T(8,128)S(1)} %bitcast.5, f32[16,7168]{1,0:T(8,128)S(1)} %copy-done.2, ...), custom_call_target="tpu_custom_call" | custom-call | tf_op jit(solution)/shard_map/reduce_update_gather/pallas_call | solution.py:411
  80.3 1.8 %copy.12 = f32[128,7168]{1,0:T(8,128)} copy(f32[128,7168]{1,0:T(8,128)S(1)} %bitcast.3) | data formatting | bytes 7340032
  82.2 0.8 copy.13
Async XLA Ops:
  0.6 2.0 %copy-start = (f32[1,1,128,7168]{3,2,1,0:T(8,128)S(1)}, f32[1,1,128,7168]{3,2,1,0:T(8,128)}, u32[]{:S(2)}) copy-start(f32[1,1,128,7168]{3,2,1,0:T(8,128)} %param.9) | copy-start | bytes 11010052
  2.7 1.0 %copy-start.1 = (f32[1,16,7168]{2,1,0:T(8,128)S(1)}, f32[1,16,7168]{2,1,0:T(8,128)}, u32[]{:S(2)}) copy-start(f32[1,16,7168]{2,1,0:T(8,128)} %param.13) | copy-start | bytes 1376260
  3.7 1.0 %copy-start.2 = (f32[16,7168]{1,0:T(8,128)S(1)}, f32[16,7168]{1,0:T(8,128)}, u32[]{:S(2)}) copy-start(f32[16,7168]{1,0:T(8,128)} %eparam.1) | copy-start | bytes 1376260
  4.7 1.0 %copy-start.3 = (f32[16,7168]{1,0:T(8,128)S(1)}, f32[16,7168]{1,0:T(8,128)}, u32[]{:S(2)}) copy-start(f32[16,7168]{1,0:T(8,128)} %efirst.1) | copy-start | bytes 1376260
  5.7 1.0 %copy-start.4 = (f32[16,7168]{1,0:T(8,128)S(1)}, f32[16,7168]{1,0:T(8,128)}, u32[]{:S(2)}) copy-start(f32[16,7168]{1,0:T(8,128)} %esecond.1) | copy-start | bytes 1376260
  6.7 0.8 copy-start.5
  7.6 0.8 copy-start.6
  8.4 0.8 copy-start.7

commit v2 on v1

v2 whole, which is shorter than its diff:
```python
import jax
import jax.numpy as jnp
from jax import lax
from jax.experimental import pallas as pl
from jax.experimental.pallas import tpu as pltpu
from jax.sharding import PartitionSpec as P

MESH = pl.DeviceIdType.MESH
D = 7168
T = 128
ORDER = (4, 3, 5, 2, 6, 1, 7, 0)
DIRECT = (3, 4)


def way(k):
    return 1 if k in (0, 1, 2, 3) else 3


class Reduce:
    def __init__(self, part, half, relays, arrived, send, peer):
        self.part, self.half, self.relays, self.arrived = part, half, relays, arrived
        self.send, self.peer = send, peer

    def start(self):
        part, half, peer, relays = self.part, self.half, self.peer, self.relays
        self.three = [self.send(part(3), relays.at[0], peer(1)), self.send(part(-3), relays.at[1], peer(7))]
        self.four = [
            self.send(half(part(4), i), half(relays.at[2], i), peer((2, 6)[i])) for i in range(2)
        ]
        self.one = [self.send(part(d), self.arrived.at[i], peer(d)) for i, d in enumerate((1, 7))]

    def relay(self):
        self.two = []
        for i, d in enumerate((2, 6)):
            mine = self.part(d)
            self.three[i].wait_recv()
            mine[...] = mine[...] + self.relays[i]
            self.four[i].wait_recv()
            more = self.half(mine, i)
            more[...] = more[...] + self.half(self.relays.at[2], i)[...]
            self.two.append(self.send(mine, self.arrived.at[2 + i], self.peer(d)))

    def finish(self):
        total = self.part(0)[...]
        for i, copy in enumerate(self.one + self.two):
            copy.wait_recv()
            total = total + self.arrived[i]
        return total


class Gather:
    def __init__(self, block, half, send, peer):
        self.block, self.half, self.send, self.peer = block, half, send, peer

    def start(self):
        mine = self.block(0)
        self.two = [self.send(mine, mine, self.peer(d)) for d in (2, 6)]
        self.one = [self.send(mine, mine, self.peer(d)) for d in (1, 7)]

    def forward(self):
        self.rest = []
        for i, d in enumerate((2, 6)):
            self.two[i].wait_recv()
            got = self.block(-d)
            self.rest.append(self.send(got, got, self.peer((1, 7)[i])))
            self.rest.append(self.send(self.half(got, i), self.half(got, i), self.peer(d)))

    def finish(self):
        for copy in self.one + self.rest:
            copy.wait_recv()


def adamw(grad, param, first, second):
    first_new = 0.9 * first + (1.0 - 0.9) * grad
    second_new = 0.95 * second + (1.0 - 0.95) * grad * grad
    step_dir = first_new / 0.19 / (jnp.sqrt(second_new / 0.0975) + 1e-08)
    return param - 0.2 * (step_dir + 0.1 * param)


def tiles(start, count):
    first = start * T
    if not isinstance(first, int):
        first = pl.multiple_of(first, T)
    return pl.ds(first, count * T)


def eight(index):
    return pl.ds(pl.multiple_of(index * 8, 8), 8)


def kernel(
    grad, param, first, second, egrad, eparam, efirst, esecond,
    out, eout,
    g_a, p_a, g_c, p_c, g_b, p_b, g_e, p_e,
    r_a1, relay_a, s_a, r_a2y, t_ay, r_a2z, t_az, r_a3,
    r_c1, relay_c, s_c, r_c2, t_c, r_c3,
    r_b1, relay_b, s_b, r_b2, r_b3,
    r_e, ep_buf, state, gathered, packed,
    load_sem, send_sem, recv_sem,
):
    rep, ep = lax.axis_index("rep"), lax.axis_index("ep")
    yh, yl = rep // 2, ep // 32
    core = rep - yh * 2
    rest = ep - yl * 32
    z = rest // 4
    x = rest - z * 4
    y = yh * 2 + yl

    def around(v, n):
        return [v] + [jnp.where(v + d >= n, v + d - n, v + d) for d in range(1, n)]

    xs, ys, zs = around(x, 4), around(y, 8), around(z, 8)
    yhs = [v // 2 for v in ys]
    yls = [yl, 1 - yl] * 4

    def x_peer(d):
        return {"rep": rep, "ep": ep + (xs[d] - x)}

    def y_peer(d):
        return {"rep": yhs[d] * 2 + core, "ep": ep + (yls[d] - yl) * 32}

    def z_peer(d):
        return {"rep": rep, "ep": ep + (zs[d] - z) * 4}

    partner = {"rep": rep + 1 - 2 * core, "ep": ep}

    barrier = pltpu.get_barrier_semaphore()
    peers = [f(d) for d in (4, 3, 5, 2, 6, 1, 7) for f in (y_peer, z_peer)]
    peers += [x_peer(d) for d in (2, 1, 3)] + [partner]
    for peer in peers:
        pl.semaphore_signal(barrier, inc=1, device_id=peer, device_id_type=MESH)

    def body(c):
        n_load, n_sem = [0], [0]
        sent, flushed = [], [0]

        def load(src, dst):
            copy = pltpu.make_async_copy(src, dst, load_sem.at[n_load[0]])
            n_load[0] += 1
            copy.start()
            return copy

        def link(src, dst, device):
            k = n_sem[0]
            n_sem[0] += 1
            return pltpu.make_async_remote_copy(
                src, dst, send_sem.at[k], recv_sem.at[k], device_id=device, device_id_type=MESH
            )

        def flush():
            for copy in sent[flushed[0]:]:
                copy.wait_send()
            flushed[0] = len(sent)

        def send(src, dst, device):
            copy = link(src, dst, device)
            copy.start()
            sent.append(copy)
            return copy

        o = 1 - c
        order = [xs[d] for d in (2, 1, 3, 0)]
        own_a = [load(grad.at[:, :, tiles(c * 16 + xx * 4, 4)], g_a.at[xx]) for xx in order]
        own_c = load(grad.at[:, :, tiles(32 + c * 8, 8)], g_c)
        own_b = load(grad.at[:, :, tiles(48 + c * 4, 4)], g_b)
        own_e = load(egrad.at[:, tiles(c * 28, 28)], g_e)
        e_cols = tiles(c * 28 + yh * 7, 7)
        own_s = [load(r, state.at[i]) for i, r in enumerate((param, first, second))]
        own_ep = [load(r.at[:, e_cols], ep_buf.at[i]) for i, r in enumerate((eparam, efirst, esecond))]
        for copy in own_s:
            copy.wait()

        pl.semaphore_wait(barrier, len(peers))

        def part(xx):
            return send(grad.at[:, :, tiles(o * 16 + xx * 4, 4)], p_a.at[xx], partner)

        part_a = [part(order[0])]
        part_c = send(grad.at[:, :, tiles(32 + o * 8, 8)], p_c, partner)
        part_b = send(grad.at[:, :, tiles(48 + o * 4, 4)], p_b, partner)
        part_e = send(egrad.at[:, tiles(o * 28, 28)], p_e, partner)
        part_a += [part(xx) for xx in order[1:]]

        def state_tiles(xx):
            jj = jnp.where(yh >= 2, yh - 2, yh)
            return (c * 16 + xx * 4 + yh, 32 + c * 8 + xx * 2 + jj, 48 + c * 4 + yh)

        state_recv = []
        for d in range(1, 4):
            for i, ct in enumerate(state_tiles(xs[d])):
                state_recv.append(send(state.at[:, :, tiles(ct, 1)], gathered.at[d, i], x_peer(d)))

        def piece(ref, k):
            k = k % 8
            if c == 0:
                return ref.at[yls[k], :, tiles(yhs[k], 1)]
            return ref.at[:, eight(zs[k]), :]

        def a_sum(i):
            own_a[i].wait()
            part_a[i].wait_recv()
            g_a[order[i]] = g_a[order[i]] + p_a[order[i]]

        a_sum(0)
        far = {k: send(piece(g_a.at[xs[2]], k), piece(relay_a, k), x_peer(way(k))) for k in ORDER}

        own_c.wait()
        part_c.wait_recv()
        g_c[...] = g_c[...] + p_c[...]
        ring_c = []
        for h in range(2):
            ring_c.append(
                Reduce(
                    lambda k, h=h: g_c.at[:, eight(zs[k % 8]), 4 * T * h : 4 * T * (h + 1)],
                    lambda ref, i: ref.at[i],
                    relay_c.at[h], r_c1.at[h], send, z_peer,
                )
            )
            ring_c[h].start()

        own_b.wait()
        part_b.wait_recv()
        g_b[...] = g_b[...] + p_b[...]
        ring_b = Reduce(
            lambda k: g_b.at[yls[k % 8], :, tiles(yhs[k % 8], 1)],
            lambda ref, i: ref.at[pl.ds(32 * i, 32), :],
            relay_b, r_b1, send, y_peer,
        )
        ring_b.start()

        own_e.wait()
        part_e.wait_recv()
        g_e[...] = g_e[...] + p_e[...]
        e1 = [
            send(g_e.at[:, tiles(yhs[2 * d] * 7, 7)], r_e.at[d - 1], y_peer(2 * d)) for d in range(1, 4)
        ]

        a_sum(1)
        a_sum(2)
        near = {1: {}, 3: {}}
        for k in ORDER:
            d = 4 - way(k)
            near[d][k] = send(piece(g_a.at[xs[d]], k), piece(r_a1.at[d // 2], k), x_peer(d))

        for k in ORDER:
            d = way(k)
            far[k].wait_recv()
            mine = piece(g_a.at[xs[d]], k)
            mine[...] = mine[...] + piece(relay_a, k)[...]
            near[d][k] = send(mine, piece(r_a1.at[d // 2], k), x_peer(d))

        ring_c[0].relay()
        ring_c[1].relay()
        ring_b.relay()
        a_sum(3)

        for copy in state_recv:
            copy.wait_recv()
        for i, ct in enumerate(state_tiles(x)):
            for d in range(4):
                row = pl.ds(2 * xs[(4 - d) % 4], 2)
                for j in range(3):
                    if d == 0:
                        packed[i, j, row, :] = state[j, :, tiles(ct, 1)]
                    else:
                        packed[i, j, row, :] = gathered[d, i, j]

        second_a, r_a2, t_a = ([], r_a2y, t_ay) if c == 0 else ([], r_a2z, t_az)
        mid_peer, last_peer = (y_peer, z_peer) if c == 0 else (z_peer, y_peer)
        for k in ORDER:
            near[1][k].wait_recv()
            near[3][k].wait_recv()
            total = piece(g_a.at[x], k)[...] + piece(r_a1.at[0], k)[...] + piece(r_a1.at[1], k)[...]
            if k:
                piece(s_a, k)[...] = total
                second_a.append(send(piece(s_a, k), r_a2.at[k - 1], mid_peer(k)))
            else:
                t_a[...] = total

        for h in range(2):
            s_c[:, :, 4 * T * h : 4 * T * (h + 1)] = ring_c[h].finish()
        c2 = [
            send(s_c.at[:, :, tiles(2 * xs[d], 2)], r_c2.at[d - 1], x_peer(d)) for d in (2, 1, 3)
        ]

        s_b[...] = ring_b.finish()
        b2 = [send(s_b.at[eight(zs[d]), :], r_b2.at[d - 1], z_peer(d)) for d in ORDER[:7]]

        for copy in e1:
            copy.wait_recv()
        for copy in own_ep:
            copy.wait()
        total = g_e[:, tiles(yh * 7, 7)]
        for d in range(1, 4):
            total = total + r_e[d - 1]
        eout[:, e_cols] = adamw(total, ep_buf[0], ep_buf[1], ep_buf[2])

        for copy in second_a:
            copy.wait_recv()
        total = t_a[...]
        for d in range(1, 8):
            total = total + r_a2[d - 1]
        t_a[...] = total
        a3 = []
        for d in ORDER[:7]:
            if c == 0:
                src = t_a.at[eight(zs[d]), :]
            else:
                src = t_a.at[yls[d], :, tiles(yhs[d], 1)]
            a3.append(send(src, r_a3.at[d - 1], last_peer(d)))

        for copy in c2:
            copy.wait_recv()
        total = s_c[:, :, tiles(2 * x, 2)]
        for d in range(1, 4):
            total = total + r_c2[d - 1]
        t_c[...] = total
        x_odd = x - 2 * (x // 2)
        halves = [v // 2 for v in yhs]
        owner = [v == x_odd for v in halves]

        c3 = []
        for d in range(1, 8):
            copy = link(t_c.at[yls[d], :, tiles(yhs[d] - 2 * halves[d], 1)], r_c3.at[d - 1], y_peer(d))
            c3.append(copy)

            @pl.when(owner[d])
            def _(copy=copy):
                copy.start()

        for copy in b2:
            copy.wait_recv()
        total = s_b[eight(z), :]
        for d in range(1, 8):
            total = total + r_b2[d - 1]
        r_b3[x] = total
        b3 = [send(r_b3.at[x], r_b3.at[x], x_peer(d)) for d in (2, 1, 3)]

        for copy in a3:
            copy.wait_recv()
        total = t_a[eight(z), :] if c == 0 else t_a[yl, :, tiles(yh, 1)]
        for d in range(1, 8):
            total = total + r_a3[d - 1]
        ct_a, ct_c, ct_b = state_tiles(x)
        tile_a = out.at[yl, eight(z), tiles(ct_a, 1)]
        tile_a[...] = adamw(total, packed[0, 0], packed[0, 1], packed[0, 2])
        a4 = [send(tile_a, tile_a, last_peer(d)) for d in ORDER[:7]]

        tile_c = out.at[yl, eight(z), tiles(ct_c, 1)]
        c4 = [link(tile_c, tile_c, y_peer(d)) for d in range(1, 8)]
        mine_c = owner[0]

        @pl.when(mine_c)
        def _():
            for copy in c3:
                copy.wait_recv()
            total = t_c[yl, :, tiles(yh - 2 * halves[0], 1)]
            for d in range(1, 8):
                total = total + r_c3[d - 1]
            tile_c[...] = adamw(total, packed[1, 0], packed[1, 1], packed[1, 2])
            for copy in c4:
                copy.start()

        tile_b = out.at[yl, eight(z), tiles(ct_b, 1)]
        for copy in b3:
            copy.wait_recv()
        total = r_b3[0] + r_b3[1] + r_b3[2] + r_b3[3]
        tile_b[...] = adamw(total, packed[2, 0], packed[2, 1], packed[2, 2])
        b5 = [send(tile_b, tile_b, z_peer(d)) for d in ORDER[:7]]

        for d in range(1, 8):
            @pl.when(owner[d])
            def _(copy=c3[d - 1]):
                copy.wait_send()

        flush()

        for copy in a4:
            copy.wait_recv()
        block_a = [out.at[:, :, tiles(c * 16 + xx * 4, 4)] for xx in xs]
        mine = piece(block_a[0], 0)
        a5 = {k: send(mine, mine, mid_peer(k)) for k in ORDER[:7]}
        done = []
        a6, a7 = {1: {}, 3: {}}, {}

        def a_out(q):
            got = piece(block_a[0], q)
            if q in DIRECT:
                a7[q] = send(got, got, x_peer(2))
            for d in (way(q), 4 - way(q)):
                a6[d][q] = send(got, got, x_peer(d))
            done.append(send(got, got, partner))

        def a_in(q):
            for d in (way(q), 4 - way(q)):
                a6[d][q].wait_recv()
                got = piece(block_a[4 - d], q)
                if q not in DIRECT and d == way(q):
                    a7[q] = send(got, got, x_peer(d))
                done.append(send(got, got, partner))

        def a_last(q):
            a7[q].wait_recv()
            got = piece(block_a[2], q)
            done.append(send(got, got, partner))

        a_out(0)

        for d in range(1, 8):
            @pl.when(owner[8 - d])
            def _(copy=c4[d - 1]):
                copy.wait_recv()
        mine = out.at[:, eight(z), tiles(32 + c * 8 + x * 2, 2)]
        c5 = {d: send(mine, mine, x_peer(d)) for d in (2, 1, 3)}
        c6 = [
            Gather(
                lambda k, xx=xx: out.at[:, eight(zs[k % 8]), tiles(32 + c * 8 + xx * 2, 2)],
                lambda ref, i: ref.at[i],
                send, z_peer,
            )
            for xx in xs
        ]
        c6[0].start()

        def c_in(d):
            c5[d].wait_recv()
            c6[4 - d].start()

        def c_last(i):
            c6[i].finish()
            got = out.at[:, :, tiles(32 + c * 8 + xs[i] * 2, 2)]
            done.append(send(got, got, partner))

        for copy in b5:
            copy.wait_recv()
        b6 = Gather(
            lambda k: out.at[yls[k % 8], :, tiles(48 + c * 4 + yhs[k % 8], 1)],
            lambda ref, i: ref.at[pl.ds(32 * i, 32), :],
            send, y_peer,
        )
        b6.start()

        e2 = [send(eout.at[:, e_cols], eout.at[:, e_cols], y_peer(2 * d)) for d in range(1, 4)]
        done.append(send(eout.at[:, e_cols], eout.at[:, e_cols], partner))

        def e_in(d):
            e2[d - 1].wait_recv()
            cols = tiles(c * 28 + yhs[8 - 2 * d] * 7, 7)
            done.append(send(eout.at[:, cols], eout.at[:, cols], partner))

        def a_mid(q):
            a5[8 - q].wait_recv()
            a_out(q)

        a_mid(7)
        a_mid(1)
        a_in(0)
        c_in(1)
        c_in(3)
        a_mid(6)
        a_mid(2)
        c_in(2)
        c6[0].forward()
        b6.forward()
        a_mid(5)
        a_mid(3)
        a_mid(4)
        a_in(7)
        a_in(1)
        c6[3].forward()
        c6[1].forward()
        a_last(0)
        a_in(6)
        a_in(2)
        c6[2].forward()
        b6.finish()
        got = out.at[:, :, tiles(48 + c * 4, 4)]
        done.append(send(got, got, partner))

        @pl.when(mine_c)
        def _():
            for copy in c4:
                copy.wait_send()

        a_last(7)
        a_last(1)
        e_in(1)
        e_in(2)
        e_in(3)
        c_last(0)
        a_in(5)
        a_in(3)
        a_in(4)
        c_last(3)
        c_last(1)
        a_last(6)
        a_last(2)
        a_last(5)
        a_last(3)
        a_last(4)
        c_last(2)

        flush()
        for copy in done:
            copy.wait_recv()

    for value in range(2):
        @pl.when(core == value)
        def _(value=value):
            body(value)


def store(out, eout, dense, expert, sem):
    copies = [pltpu.make_async_copy(out.at[i], dense.at[i], sem.at[i]) for i in range(2)]
    copies.append(pltpu.make_async_copy(eout, expert, sem.at[2]))
    for copy in copies:
        copy.start()
    for copy in copies:
        copy.wait()


def shards(grad, param, first, second, egrad, eparam, efirst, esecond):
    vmem = lambda *shape: pltpu.VMEM(shape, jnp.float32)
    block = (2, 64, 4 * T)
    out, eout = pl.pallas_call(
        kernel,
        out_shape=(vmem(2, 64, D), vmem(16, D)),
        in_specs=[pl.BlockSpec(memory_space=pltpu.HBM)] * 8,
        out_specs=(pl.BlockSpec(memory_space=pltpu.VMEM),) * 2,
        scratch_shapes=[
            vmem(4, *block), vmem(4, *block), vmem(2, 64, 8 * T), vmem(2, 64, 8 * T), vmem(*block), vmem(*block),
            vmem(16, 28 * T), vmem(16, 28 * T),
            vmem(2, *block), vmem(*block), vmem(*block), vmem(7, 64, T), vmem(64, T), vmem(7, 2, 8, 4 * T), vmem(2, 8, 4 * T), vmem(7, 8, T),
            vmem(2, 4, 2, 8, 4 * T), vmem(2, 3, 2, 8, 4 * T), vmem(2, 8, 8 * T), vmem(3, 2, 8, 2 * T), vmem(2, 8, 2 * T), vmem(7, 8, T),
            vmem(4, 64, T), vmem(3, 64, T), vmem(64, T), vmem(7, 8, T), vmem(4, 8, T),
            vmem(3, 16, 7 * T), vmem(3, 16, 7 * T), vmem(3, 2, D), vmem(4, 3, 3, 2, T), vmem(3, 3, 8, T),
            pltpu.SemaphoreType.DMA((16,)),
            pltpu.SemaphoreType.DMA((320,)),
            pltpu.SemaphoreType.DMA((320,)),
        ],
        compiler_params=pltpu.CompilerParams(
            collective_id=0, has_side_effects=True, vmem_limit_bytes=40 * 1024 * 1024
        ),
        name="reduce_update_gather",
    )(
        *(
            pltpu.with_memory_space_constraint(a, pltpu.HBM)
            for a in (grad.reshape(2, 64, D), param, first, second, egrad.reshape(16, D), eparam, efirst, esecond)
        )
    )
    dense, expert = pl.pallas_call(
        store,
        out_shape=(
            jax.ShapeDtypeStruct((2, 64, D), jnp.float32),
            jax.ShapeDtypeStruct((16, D), jnp.float32),
        ),
        in_specs=[pl.BlockSpec(memory_space=pltpu.VMEM)] * 2,
        out_specs=(pl.BlockSpec(memory_space=pltpu.HBM),) * 2,
        scratch_shapes=[pltpu.SemaphoreType.DMA((3,))],
        compiler_params=pltpu.CompilerParams(vmem_limit_bytes=16 * 1024 * 1024),
        name="store",
    )(*(pltpu.with_memory_space_constraint(a, pltpu.VMEM) for a in (out, eout)))
    return dense.reshape(128, D), expert


def solution(mesh):
    placed = (
        P("rep", "ep", None, None),
        P("ep", None),
        P("ep", None),
        P("ep", None),
        P("rep", "ep", None),
        P("ep", None),
        P("ep", None),
        P("ep", None),
    )
    return jax.shard_map(
        shards, mesh=mesh, in_specs=placed, out_specs=(P(), P("ep", None)), check_vma=False
    )
```

time: 83.4 us -> 68.3 us (0.82)
  local copies, waits for them, and re-layouts: 11.2 us -> 0 us
  Pallas kernels: 71.1 us -> 67.5 us
    unnamed x18 -> x0, local copies, waits for them, and re-layouts: 11.2 us -> none
    pallas_call x1 -> x2, Pallas kernels: 71.1 us -> 67.5 us  [the longest x1 65.5 us: shards(): pl.pallas_call(kernel, out_shape=(vmem(2, 64, D), vmem(16, D)), in_specs=...]
where the time goes in v2:
time: 68.3 us; the launch traced here: 68.1 us
  Pallas kernels  67.5 us (99%)
    pallas_call x1, Pallas kernels, shards(): pl.pallas_call(kernel, out_shape=(vmem(2, 64, D), vmem(16, D)), in_specs=...  65.5 us
    pallas_call x1, Pallas kernels, shards(): pl.pallas_call(store, out_shape=(jax.ShapeDtypeStruct((2, 64, D), jnp.flo...  2 us

profile of v2, /device:TPU:1, one launch (start us, length us, event | category | flops | bytes accessed | tf_op | source)
XLA Modules:
  0.0 68.1 jit_solution(4870507503405574805)
XLA Ops:
  0.6 65.5 %reduce_update_gather.1 = (f32[2,64,7168]{2,1,0:T(8,128)S(1)}, f32[16,7168]{1,0:T(8,128)S(1)}) custom-call(f32[2,64,7168]{2,1,0:T(8,128)} %bitcast.3, f32[2,7168]{1,0:T(2,128)} %param.17, f32[2,7168]{1,0:T(2,128)} %first.1, f32[2,7168]{1,0:T(2,128)} %second.1, f32[16,7168]{1,0:T(8,128)} %bitcast.4, f32[16,7168]{1,0:T(8,128)} %eparam.1, f32[16,7168]{1,0:T(8,128)} %efirst.1, ...), custom_call_target="tpu_custom_call" | custom-call | tf_op jit(solution)/shard_map/reduce_update_gather/pallas_call | solution.py:525
  66.1 2.0 %store.1 = (f32[2,64,7168]{2,1,0:T(8,128)}, f32[16,7168]{1,0:T(8,128)}) custom-call(f32[2,64,7168]{2,1,0:T(8,128)S(1)} %get-tuple-element.6.out, f32[16,7168]{1,0:T(8,128)S(1)} %get-tuple-element.7.eout), custom_call_target="tpu_custom_call" | custom-call | tf_op jit(solution)/shard_map/store/pallas_call | solution.py:551

commit v3 on v2

--- a/solution.py
+++ b/solution.py
@@ -9,7 +9,7 @@
 D = 7168
 T = 128
 ORDER = (4, 3, 5, 2, 6, 1, 7, 0)
-DIRECT = (3, 4)
+DIRECT = (0, 1, 2, 3, 4, 5, 6, 7)
 
 
 def way(k):
@@ -51,14 +51,21 @@
 class Gather:
     def __init__(self, block, half, send, peer):
         self.block, self.half, self.send, self.peer = block, half, send, peer
+        self.straight = peer.__name__ in ('z_peer',)
 
     def start(self):
         mine = self.block(0)
+        self.all = {}
+        if self.straight:
+            self.all = {d: self.send(mine, mine, self.peer(d)) for d in (1, 7, 2, 6, 3, 5, 4)}
+            return
         self.two = [self.send(mine, mine, self.peer(d)) for d in (2, 6)]
         self.one = [self.send(mine, mine, self.peer(d)) for d in (1, 7)]
 
     def forward(self):
         self.rest = []
+        if self.straight:
+            return
         for i, d in enumerate((2, 6)):
             self.two[i].wait_recv()
             got = self.block(-d)
@@ -66,6 +73,10 @@
             self.rest.append(self.send(self.half(got, i), self.half(got, i), self.peer(d)))
 
     def finish(self):
+        if self.straight:
+            for copy in self.all.values():
+                copy.wait_recv()
+            return
         for copy in self.one + self.rest:
             copy.wait_recv()
 
@@ -96,7 +107,7 @@
     r_c1, relay_c, s_c, r_c2, t_c, r_c3,
     r_b1, relay_b, s_b, r_b2, r_b3,
     r_e, ep_buf, state, gathered, packed,
-    load_sem, send_sem, recv_sem,
+    load_sem, send_sem, recv_sem, passed,
 ):
     rep, ep = lax.axis_index("rep"), lax.axis_index("ep")
     yh, yl = rep // 2, ep // 32
@@ -125,9 +136,9 @@
     partner = {"rep": rep + 1 - 2 * core, "ep": ep}
 
     barrier = pltpu.get_barrier_semaphore()
-    peers = [f(d) for d in (4, 3, 5, 2, 6, 1, 7) for f in (y_peer, z_peer)]
-    peers += [x_peer(d) for d in (2, 1, 3)] + [partner]
-    for peer in peers:
+    near_peers = [f(d) for d in (2, 6, 1, 7) for f in (y_peer, z_peer)]
+    near_peers += [x_peer(d) for d in (2, 1, 3)] + [partner]
+    for peer in near_peers:
         pl.semaphore_signal(barrier, inc=1, device_id=peer, device_id_type=MESH)
 
     def body(c):
@@ -170,7 +181,9 @@
         for copy in own_s:
             copy.wait()
 
-        pl.semaphore_wait(barrier, len(peers))
+        pl.semaphore_wait(barrier, len(near_peers))
+        for peer in near_peers[:8]:
+            pl.semaphore_signal(passed, inc=1, device_id=peer, device_id_type=MESH)
 
         def part(xx):
             return send(grad.at[:, :, tiles(o * 16 + xx * 4, 4)], p_a.at[xx], partner)
@@ -228,6 +241,8 @@
         )
         ring_b.start()
 
+        pl.semaphore_wait(passed, 8)
+
         own_e.wait()
         part_e.wait_recv()
         g_e[...] = g_e[...] + p_e[...]
@@ -375,12 +390,15 @@
 
         flush()
 
+        done = []
+        e2 = [send(eout.at[:, e_cols], eout.at[:, e_cols], y_peer(2 * d)) for d in range(1, 4)]
+        done.append(send(eout.at[:, e_cols], eout.at[:, e_cols], partner))
+
         for copy in a4:
             copy.wait_recv()
         block_a = [out.at[:, :, tiles(c * 16 + xx * 4, 4)] for xx in xs]
         mine = piece(block_a[0], 0)
-        a5 = {k: send(mine, mine, mid_peer(k)) for k in ORDER[:7]}
-        done = []
+        a5 = {k: send(mine, mine, mid_peer(k)) for k in (1, 7, 2, 6, 3, 5, 4)}
         a6, a7 = {1: {}, 3: {}}, {}
 
         def a_out(q):
@@ -439,9 +457,6 @@
             send, y_peer,
         )
         b6.start()
-
-        e2 = [send(eout.at[:, e_cols], eout.at[:, e_cols], y_peer(2 * d)) for d in range(1, 4)]
-        done.append(send(eout.at[:, e_cols], eout.at[:, e_cols], partner))
 
         def e_in(d):
             e2[d - 1].wait_recv()
@@ -537,6 +552,7 @@
             pltpu.SemaphoreType.DMA((16,)),
             pltpu.SemaphoreType.DMA((320,)),
             pltpu.SemaphoreType.DMA((320,)),
+            pltpu.SemaphoreType.REGULAR,
         ],
         compiler_params=pltpu.CompilerParams(
             collective_id=0, has_side_effects=True, vmem_limit_bytes=40 * 1024 * 1024

time: 68.3 us -> 65.1 us (0.953)
  Pallas kernels: 67.5 us -> 64.3 us
    pallas_call x1, Pallas kernels: 65.5 us -> 62.3 us  [shards(): pl.pallas_call(kernel, out_shape=(vmem(2, 64, D), vmem(16, D)), in_specs=...]
where the time goes in v3:
time: 65.1 us; the launch traced here: 65 us
  Pallas kernels  64.3 us (99%)
    pallas_call x1, Pallas kernels, shards(): pl.pallas_call(kernel, out_shape=(vmem(2, 64, D), vmem(16, D)), in_specs=...  62.3 us
    pallas_call x1, Pallas kernels, shards(): pl.pallas_call(store, out_shape=(jax.ShapeDtypeStruct((2, 64, D), jnp.flo...  2 us

profile of v3, /device:TPU:1, one launch (start us, length us, event | category | flops | bytes accessed | tf_op | source)
XLA Modules:
  0.0 65.0 jit_solution(428446146603845613)
XLA Ops:
  0.6 62.3 %reduce_update_gather.1 = (f32[2,64,7168]{2,1,0:T(8,128)S(1)}, f32[16,7168]{1,0:T(8,128)S(1)}) custom-call(f32[2,64,7168]{2,1,0:T(8,128)} %bitcast.3, f32[2,7168]{1,0:T(2,128)} %param.17, f32[2,7168]{1,0:T(2,128)} %first.1, f32[2,7168]{1,0:T(2,128)} %second.1, f32[16,7168]{1,0:T(8,128)} %bitcast.4, f32[16,7168]{1,0:T(8,128)} %eparam.1, f32[16,7168]{1,0:T(8,128)} %efirst.1, ...), custom_call_target="tpu_custom_call" | custom-call | tf_op jit(solution)/shard_map/reduce_update_gather/pallas_call | solution.py:540
  63.0 2.0 %store.1 = (f32[2,64,7168]{2,1,0:T(8,128)}, f32[16,7168]{1,0:T(8,128)}) custom-call(f32[2,64,7168]{2,1,0:T(8,128)S(1)} %get-tuple-element.6.out, f32[16,7168]{1,0:T(8,128)S(1)} %get-tuple-element.7.eout), custom_call_target="tpu_custom_call" | custom-call | tf_op jit(solution)/shard_map/store/pallas_call | solution.py:567

commit v4 on v3

--- a/solution.py
+++ b/solution.py
@@ -301,15 +301,6 @@
         s_b[...] = ring_b.finish()
         b2 = [send(s_b.at[eight(zs[d]), :], r_b2.at[d - 1], z_peer(d)) for d in ORDER[:7]]
 
-        for copy in e1:
-            copy.wait_recv()
-        for copy in own_ep:
-            copy.wait()
-        total = g_e[:, tiles(yh * 7, 7)]
-        for d in range(1, 4):
-            total = total + r_e[d - 1]
-        eout[:, e_cols] = adamw(total, ep_buf[0], ep_buf[1], ep_buf[2])
-
         for copy in second_a:
             copy.wait_recv()
         total = t_a[...]
@@ -342,6 +333,15 @@
             @pl.when(owner[d])
             def _(copy=copy):
                 copy.start()
+
+        for copy in e1:
+            copy.wait_recv()
+        for copy in own_ep:
+            copy.wait()
+        total = g_e[:, tiles(yh * 7, 7)]
+        for d in range(1, 4):
+            total = total + r_e[d - 1]
+        eout[:, e_cols] = adamw(total, ep_buf[0], ep_buf[1], ep_buf[2])
 
         for copy in b2:
             copy.wait_recv()
@@ -476,42 +476,41 @@
         a_mid(2)
         c_in(2)
         c6[0].forward()
+        c6[1].forward()
+        c6[2].forward()
+        c6[3].forward()
         b6.forward()
         a_mid(5)
         a_mid(3)
         a_mid(4)
-        a_in(7)
-        a_in(1)
-        c6[3].forward()
-        c6[1].forward()
-        a_last(0)
-        a_in(6)
-        a_in(2)
-        c6[2].forward()
-        b6.finish()
-        got = out.at[:, :, tiles(48 + c * 4, 4)]
-        done.append(send(got, got, partner))
-
         @pl.when(mine_c)
         def _():
             for copy in c4:
                 copy.wait_send()
 
+        a_last(0)
+        a_in(7)
         a_last(7)
+        a_in(1)
         a_last(1)
         e_in(1)
         e_in(2)
         e_in(3)
+        b6.finish()
+        got = out.at[:, :, tiles(48 + c * 4, 4)]
+        done.append(send(got, got, partner))
+        a_in(6)
+        a_last(6)
         c_last(0)
+        a_in(2)
+        a_last(2)
+        c_last(3)
         a_in(5)
+        a_last(5)
+        c_last(1)
         a_in(3)
+        a_last(3)
         a_in(4)
-        c_last(3)
-        c_last(1)
-        a_last(6)
-        a_last(2)
-        a_last(5)
-        a_last(3)
         a_last(4)
         c_last(2)
 

time: 65.1 us -> 64.8 us (level)
  no operation moved by 1% of the time
where the time goes in v4:
time: 64.8 us; the launch traced here: 64.7 us
  Pallas kernels  64 us (99%)
    pallas_call x1, Pallas kernels, shards(): pl.pallas_call(kernel, out_shape=(vmem(2, 64, D), vmem(16, D)), in_specs=...  62 us
    pallas_call x1, Pallas kernels, shards(): pl.pallas_call(store, out_shape=(jax.ShapeDtypeStruct((2, 64, D), jnp.flo...  2 us

profile of v4, /device:TPU:1, one launch (start us, length us, event | category | flops | bytes accessed | tf_op | source)
XLA Modules:
  0.0 64.7 jit_solution(6853705662460325929)
XLA Ops:
  0.6 62.0 %reduce_update_gather.1 = (f32[2,64,7168]{2,1,0:T(8,128)S(1)}, f32[16,7168]{1,0:T(8,128)S(1)}) custom-call(f32[2,64,7168]{2,1,0:T(8,128)} %bitcast.3, f32[2,7168]{1,0:T(2,128)} %param.17, f32[2,7168]{1,0:T(2,128)} %first.1, f32[2,7168]{1,0:T(2,128)} %second.1, f32[16,7168]{1,0:T(8,128)} %bitcast.4, f32[16,7168]{1,0:T(8,128)} %eparam.1, f32[16,7168]{1,0:T(8,128)} %efirst.1, ...), custom_call_target="tpu_custom_call" | custom-call | tf_op jit(solution)/shard_map/reduce_update_gather/pallas_call | solution.py:539
  62.7 2.0 %store.1 = (f32[2,64,7168]{2,1,0:T(8,128)}, f32[16,7168]{1,0:T(8,128)}) custom-call(f32[2,64,7168]{2,1,0:T(8,128)S(1)} %get-tuple-element.6.out, f32[16,7168]{1,0:T(8,128)S(1)} %get-tuple-element.7.eout), custom_call_target="tpu_custom_call" | custom-call | tf_op jit(solution)/shard_map/store/pallas_call | solution.py:566
